TPU v7x, 32 devices: a whole 2x2x4 slice. The times are simulated.
32 devices in a mesh: region: 2 (over x), graph: 16 (over z, y, core).
Axes of the slice: x: 2, y: 2, z: 4, core: 2. Of those that a mesh axis runs over, the one named last changes fastest.
Arguments:
- observed: float32 [96, 256, 128], P(None, ('region', 'graph')), parts along dimension 1, may hold values from -6 to 6
- mask: int32 [96, 256, 128], P(None, ('region', 'graph')), parts along dimension 1, may hold values 0 or 1
- first_guess: float32 [96, 256, 128], P(None, ('region', 'graph')), parts along dimension 1, may hold values from -4 to 4
- diag_weight: float32 [256, 128], P(('region', 'graph')), parts along dimension 0, may hold values from 0.2 to 2
- coupling: bfloat16 [256, 5, 128, 128], P(('region', 'graph')), parts along dimension 0, may hold values from 0 to 0.0015563965
- block_cols: int32 [256, 5], P(('region', 'graph')), parts along dimension 0, may hold values from 0 to 23, as said below
- send_rows: int32 [32, 4, 4], P(('region', 'graph')), parts along dimension 0, may hold values from 0 to 7, as said below
Outputs:
- solution_field: float32 [96, 256, 128], P(None, ('region', 'graph')), parts along dimension 1
- residual: float32 [96, 256, 128], P(None, ('region', 'graph')), parts along dimension 1
There are 2 independent parts, one for each index of `region`. A program takes and returns all parts, laid end to end along the dimension named above; each array names one. Nothing has to cross between parts.
Inputs may be any that keep to these rules, and one draw needn't show every extreme that they name: `block_cols`: slot 0 of block row i is the row's own block i modulo 8; the other slots are any of the 24 extended blocks. `send_rows`: the 4 entries of one partition and offset are distinct own blocks.
All inputs are finite; a program needn't handle non-finite values. No bound on the sum of `mask` on one device may be relied on, other than what follows from the above.
Results may differ from a plain program's by a relative error of at most 0.0003.
Values sent between devices are 32-bit elements; how exact they have to be, the bound alone decides.
A program may use at most 64 MiB of HBM per device.

v0:
```python
import jax
import jax.numpy as jnp
from jax import lax
from jax.sharding import PartitionSpec as P

ITERS = 2


OFFSETS = (1, -1, 2, -2)
time_tie = 0.5


def shifted(block, axis, distance):
    devices = range(lax.axis_size(axis))
    route = [(i - distance, i) for i in devices if i - distance in devices]
    return lax.ppermute(block, axis, route)


def block_product(form, weights, field):
    upper = field.astype(jnp.bfloat16)
    lower = (field - upper.astype(jnp.float32)).astype(jnp.bfloat16)
    first = jnp.einsum(form, weights, upper, preferred_element_type=jnp.float32)
    return first + jnp.einsum(form, weights, lower, preferred_element_type=jnp.float32)


def deliver(parcels):
    arrived = {}
    for offset in OFFSETS:
        arrived[offset] = shifted(parcels[offset], "graph", offset)
    return arrived


def forward_parcels(field, send_list):
    return {offset: field[:, send_list[index]] for index, offset in enumerate(OFFSETS)}


def forward_finish(field, weights, column_ids, arrived):
    extended = jnp.concatenate([field] + [arrived[offset] for offset in OFFSETS], axis=1)
    gathered = jnp.take(extended, column_ids, axis=1)
    gathered = gathered.reshape(field.shape[0], weights.shape[0], weights.shape[1], field.shape[2])
    return block_product("bkrc,tbkc->tbr", weights, gathered)


def transpose_collect(field, weights, column_ids, ext_count):
    terms = block_product("bkrc,tbr->tbkc", weights, field)
    terms = terms.reshape(field.shape[0], -1, field.shape[2])
    blank = jnp.zeros((field.shape[0], ext_count, field.shape[2]), jnp.float32)
    return blank.at[:, column_ids].add(terms)


def transpose_parcels(collected, own_count, capacity):
    parcels = {}
    for index, offset in enumerate(OFFSETS):
        start = own_count + index * capacity
        parcels[-offset] = collected[:, start : start + capacity]
    return parcels


def transpose_finish(collected, own_count, send_list, arrived):
    total = collected[:, :own_count]
    for index, offset in enumerate(OFFSETS):
        total = total.at[:, send_list[index]].add(arrived[-offset])
    return total


def time_laplace(field):
    before = jnp.concatenate([field[:1], field[:-1]], axis=0)
    after = jnp.concatenate([field[1:], field[-1:]], axis=0)
    return 2.0 * field - before - after


def squares_sum(residual):
    return lax.psum(jnp.sum(residual * residual), "graph")


def per_device(observed, mask, first_guess, diag_weight, coupling, block_cols, send_rows):
    own_count = observed.shape[1]
    send_list = send_rows[0]
    capacity = send_list.shape[1]
    ext_count = own_count + 4 * capacity
    column_ids = block_cols.reshape(-1)

    def transposed(field):
        collected = transpose_collect(field, coupling, column_ids, ext_count)
        arrived = deliver(transpose_parcels(collected, own_count, capacity))
        return transpose_finish(collected, own_count, send_list, arrived)

    unit_field = jnp.ones((1, own_count, observed.shape[2]), jnp.float32)
    row_part = jnp.sum(coupling.astype(jnp.float32), axis=(1, 3))
    degree = row_part + transposed(unit_field)[0]
    mask_f = mask.astype(jnp.float32)
    diagonal = mask_f + diag_weight[None] + degree[None]

    def coupled_of(field):
        arrived = deliver(forward_parcels(field, send_list))
        return forward_finish(field, coupling, column_ids, arrived) + transposed(field)

    def operate(field):
        return diagonal * field - coupled_of(field) + time_tie * time_laplace(field)

    right_side = mask_f * observed
    solution_field = first_guess
    residual = right_side - operate(first_guess)
    direction = residual
    norm_now = squares_sum(residual)
    for step in range(ITERS):
        image = operate(direction)
        step_size = norm_now / lax.psum(jnp.sum(direction * image), "graph")
        solution_field = solution_field + step_size * direction
        residual = residual - step_size * image
        norm_next = squares_sum(residual)
        direction = residual + norm_next / norm_now * direction
        norm_now = norm_next
    return (solution_field, residual)


def solution(mesh):
    placed = (
        P(None, ("region", "graph"), None),
        P(None, ("region", "graph"), None),
        P(None, ("region", "graph"), None),
        P(("region", "graph"), None),
        P(("region", "graph"), None, None, None),
        P(("region", "graph"), None),
        P(("region", "graph"), None, None),
    )
    return jax.shard_map(
        per_device,
        mesh=mesh,
        in_specs=placed,
        out_specs=(P(None, ("region", "graph"), None), P(None, ("region", "graph"), None)),
        check_vma=False,
    )
```

profile of v0, /device:TPU:0, one launch (start us, length us, event | category | flops | bytes accessed | tf_op | source)
XLA Modules:
  0.0 314.3 jit_solution(11950309665281743836)
XLA Ops:
  1.5 2.7 gather_fusion
  4.1 3.2 %collective-permute-start.4 = (f32[96,4,128]{2,1,0:T(4,128)}, f32[96,4,128]{2,1,0:T(4,128)}, u32[]{:S(2)}, u32[]{:S(2)}) collective-permute-start(f32[96,4,128]{2,1,0:T(4,128)} %bitcast.18), channel_id=1, source_target_pairs={{0,1},{1,2},{2,3},{3,4},{4,5},{5,6},{6,7},{7,8},{8,9},{9,10},{10,1... | collective-permute-start | bytes 589832 | tf_op jit(solution)/shard_map/ppermute | solution.py:16
  10.7 4.5 %collective-permute-start.1 = (f32[1,4,128]{2,1,0:T(4,128)}, f32[1,4,128]{2,1,0:T(4,128)S(1)}, u32[]{:S(2)}, u32[]{:S(2)}) collective-permute-start(f32[1,4,128]{2,1,0:T(4,128)} %get-tuple-element.48), channel_id=1, source_target_pairs={{0,1},{1,2},{2,3},{3,4},{4,5},{5,6},{6,7},{7,8},{8,9},{9,10},{10,1... | collective-permute-start | bytes 6152 | tf_op jit(solution)/shard_map/ppermute | solution.py:16
  16.5 4.5 %collective-permute-start.3 = (f32[1,4,128]{2,1,0:T(4,128)}, f32[1,4,128]{2,1,0:T(4,128)S(1)}, u32[]{:S(2)}, u32[]{:S(2)}) collective-permute-start(f32[1,4,128]{2,1,0:T(4,128)} %get-tuple-element.46), channel_id=1, source_target_pairs={{0,2},{1,3},{2,4},{3,5},{4,6},{5,7},{6,8},{7,9},{8,10},{9,11},{10,... | collective-permute-start | bytes 6152 | tf_op jit(solution)/shard_map/ppermute | solution.py:16
  25.9 6.0 %scatter_fusion = f32[96,24,128]{2,0,1:T(8,128)S(1)} fusion(f32[96,24,128]{2,0,1:T(8,128)S(1)} %broadcast.101.clone, s32[40]{0:T(128)S(1)} %fusion.56, f32[40,96,128]{2,1,0:T(8,128)} %bitcast.181), kind=kCustom, calls=%fused_computation.20 | custom fusion | flops 491520 | bytes 5898400 | tf_op jit(solution)/shard_map/scatter-add | solution.py:48
  42.4 6.0 %collective-permute-start.6 = (f32[96,4,128]{2,1,0:T(4,128)}, f32[96,4,128]{2,1,0:T(4,128)S(1)}, u32[]{:S(2)}, u32[]{:S(2)}) collective-permute-start(f32[96,4,128]{2,1,0:T(4,128)} %bitcast.190), channel_id=1, source_target_pairs={{0,2},{1,3},{2,4},{3,5},{4,6},{5,7},{6,8},{7,9},{8,10},{9,11},{10,... | collective-permute-start | bytes 589832 | tf_op jit(solution)/shard_map/ppermute | solution.py:16
  52.9 3.9 %collective-permute-start.9 = (f32[96,4,128]{2,0,1:T(8,128)}, f32[96,4,128]{2,0,1:T(8,128)}, u32[]{:S(2)}, u32[]{:S(2)}) collective-permute-start(f32[96,4,128]{2,0,1:T(8,128)} %get-tuple-element.28), channel_id=1, source_target_pairs={{0,1},{1,2},{2,3},{3,4},{4,5},{5,6},{6,7},{7,8},{8,9},{9,10},{10,1... | collective-permute-start | bytes 589832 | tf_op jit(solution)/shard_map/ppermute | solution.py:16
  60.4 6.5 %collective-permute-start.11 = (f32[96,4,128]{2,0,1:T(8,128)S(1)}, f32[96,4,128]{2,0,1:T(8,128)}, u32[]{:S(2)}, u32[]{:S(2)}) collective-permute-start(f32[96,4,128]{2,0,1:T(8,128)S(1)} %get-tuple-element.26), channel_id=1, source_target_pairs={{0,2},{1,3},{2,4},{3,5},{4,6},{5,7},{6,8},{7,9},{8,10},{9,11},{10,... | collective-permute-start | bytes 589832 | tf_op jit(solution)/shard_map/ppermute | solution.py:16
  69.2 3.2 %gather_fusion.12 = f32[40,96,128]{2,1,0:T(8,128)} fusion(f32[96,24,128]{2,0,1:T(8,128)} %copy_dynamic-update-slice_fusion, s32[1024]{0:T(1024)S(1)} %pad_clamp_fusion), kind=kCustom, calls=%fused_computation.clone | custom fusion | bytes 3932320 | tf_op jit(solution)/shard_map/jit(_take)/gather | solution.py:39
  82.0 2.2 constant_dynamic-update-slice_fusion.5
  89.3 3.2 %convolution_add_fusion.1 = f32[8,96,5,128]{3,1,2,0:T(8,128)} fusion(f32[8,96,5,128]{3,1,2,0:T(8,128)} %fusion.32, bf16[8,5,128,128]{3,2,1,0:T(8,128)(2,1)S(1)} %copy-done, f32[96,8,128]{2,0,1:T(8,128)S(1)} %get-tuple-element.17), kind=kOutput, calls=%fused_computation.40 | convolution fusion | flops 126713856 | bytes 5636096 | tf_op jit(solution)/shard_map/bkrc,tbr->tbkc/dot_general | solution.py:23
  92.7 6.0 %scatter_fusion.5 = f32[96,24,128]{2,0,1:T(8,128)S(1)} fusion(f32[96,24,128]{2,0,1:T(8,128)S(1)} %broadcast.101.clone.1, s32[40]{0:T(128)S(1)} %fusion.56, f32[40,96,128]{2,1,0:T(8,128)} %bitcast.183), kind=kCustom, calls=%fused_computation.25 | custom fusion | flops 491520 | bytes 5898400 | tf_op jit(solution)/shard_map/scatter-add | solution.py:48
  99.5 4.8 %collective-permute-start.12 = (f32[96,4,128]{2,0,1:T(8,128)}, f32[96,4,128]{2,0,1:T(8,128)}, u32[]{:S(2)}, u32[]{:S(2)}) collective-permute-start(f32[96,4,128]{2,0,1:T(8,128)} %bitcast.41), channel_id=1, source_target_pairs={{0,1},{1,2},{2,3},{3,4},{4,5},{5,6},{6,7},{7,8},{8,9},{9,10},{10,1... | collective-permute-start | bytes 589832 | tf_op jit(solution)/shard_map/ppermute | solution.py:16
  109.4 5.3 %collective-permute-start.14 = (f32[96,4,128]{2,0,1:T(8,128)}, f32[96,4,128]{2,0,1:T(8,128)S(1)}, u32[]{:S(2)}, u32[]{:S(2)}) collective-permute-start(f32[96,4,128]{2,0,1:T(8,128)} %bitcast.188), channel_id=1, source_target_pairs={{0,2},{1,3},{2,4},{3,5},{4,6},{5,7},{6,8},{7,9},{8,10},{9,11},{10,... | collective-permute-start | bytes 589832 | tf_op jit(solution)/shard_map/ppermute | solution.py:16
  122.5 2.4 collective-permute-done.14
  124.9 5.0 %collective-permute-start.19 = (f32[96,4,128]{2,0,1:T(8,128)S(1)}, f32[96,4,128]{2,0,1:T(8,128)}, u32[]{:S(2)}, u32[]{:S(2)}) collective-permute-start(f32[96,4,128]{2,0,1:T(8,128)S(1)} %get-tuple-element.22), channel_id=1, source_target_pairs={{0,2},{1,3},{2,4},{3,5},{4,6},{5,7},{6,8},{7,9},{8,10},{9,11},{10,... | collective-permute-start | bytes 589832 | tf_op jit(solution)/shard_map/ppermute | solution.py:16
  131.3 3.2 %gather_fusion.13 = f32[40,96,128]{2,1,0:T(8,128)} fusion(f32[96,24,128]{2,0,1:T(8,128)} %constant_dynamic-update-slice_fusion.1, s32[1024]{0:T(1024)S(1)} %pad_clamp_fusion), kind=kCustom, calls=%fused_computation.1.clone | custom fusion | bytes 3932320 | tf_op jit(solution)/shard_map/jit(_take)/gather | solution.py:39
  138.3 2.4 scatter_fusion.6
  140.7 2.4 scatter_fusion.7
  143.0 2.3 scatter_fusion.8
  145.4 2.4 scatter_fusion.9
  147.7 2.0 multiply_reduce_fusion.2
  149.8 32.7 %all-reduce = (f32[]{:T(128)}, f32[]{:T(128)}) all-reduce(f32[]{:T(128)} %get-tuple-element.8, f32[]{:T(128)} %get-tuple-element.7), channel_id=1, replica_groups=mesh['region'=2,'graph'=16] {'graph'}, use_global_device_ids=true, to_apply=%region_12.14 | all-reduce | flops 2 | bytes 16 | tf_op jit(solution)/shard_map/psum | solution.py:73
  184.5 30.1 %psum.30 = f32[]{:T(128)} all-reduce(f32[]{:T(128)} %multiply_reduce_fusion.1), channel_id=1, replica_groups=mesh['region'=2,'graph'=16] {'graph'}, use_global_device_ids=true, to_apply=%region_21.23 | all-reduce | flops 1 | bytes 8 | tf_op jit(solution)/shard_map/psum | solution.py:73
  221.2 3.2 %convolution_add_fusion = f32[8,96,5,128]{3,1,2,0:T(8,128)} fusion(f32[8,96,5,128]{3,1,2,0:T(8,128)} %fusion.30, bf16[8,5,128,128]{3,2,1,0:T(8,128)(2,1)S(1)} %copy-done, f32[96,8,128]{2,0,1:T(8,128)S(1)} %get-tuple-element.14), kind=kOutput, calls=%fused_computation.39 | convolution fusion | flops 126713856 | bytes 5636096 | tf_op jit(solution)/shard_map/bkrc,tbr->tbkc/dot_general | solution.py:23
  225.7 8.7 %scatter_fusion.10 = f32[96,24,128]{2,0,1:T(8,128)} fusion(f32[96,24,128]{2,0,1:T(8,128)} %broadcast.101, s32[40]{0:T(128)S(1)} %fusion.56, f32[40,96,128]{2,1,0:T(8,128)} %bitcast.182), kind=kCustom, calls=%fused_computation.30 | custom fusion | flops 491520 | bytes 5898400 | tf_op jit(solution)/shard_map/scatter-add | solution.py:48
  234.3 2.1 fusion.66
  236.4 2.5 collective-permute-start.20
  243.3 5.3 %collective-permute-start.22 = (f32[96,4,128]{2,0,1:T(8,128)}, f32[96,4,128]{2,0,1:T(8,128)S(1)}, u32[]{:S(2)}, u32[]{:S(2)}) collective-permute-start(f32[96,4,128]{2,0,1:T(8,128)} %bitcast.187), channel_id=1, source_target_pairs={{0,2},{1,3},{2,4},{3,5},{4,6},{5,7},{6,8},{7,9},{8,10},{9,11},{10,... | collective-permute-start | bytes 589832 | tf_op jit(solution)/shard_map/ppermute | solution.py:16
  258.2 5.0 %collective-permute-start.27 = (f32[96,4,128]{2,0,1:T(8,128)S(1)}, f32[96,4,128]{2,0,1:T(8,128)}, u32[]{:S(2)}, u32[]{:S(2)}) collective-permute-start(f32[96,4,128]{2,0,1:T(8,128)S(1)} %get-tuple-element.18), channel_id=1, source_target_pairs={{0,2},{1,3},{2,4},{3,5},{4,6},{5,7},{6,8},{7,9},{8,10},{9,11},{10,... | collective-permute-start | bytes 589832 | tf_op jit(solution)/shard_map/ppermute | solution.py:16
  264.6 3.2 %gather_fusion.14 = f32[40,96,128]{2,1,0:T(8,128)} fusion(f32[96,24,128]{2,0,1:T(8,128)} %constant_dynamic-update-slice_fusion.6, s32[1024]{0:T(1024)S(1)} %pad_clamp_fusion), kind=kCustom, calls=%fused_computation.2.clone | custom fusion | bytes 3932320 | tf_op jit(solution)/shard_map/jit(_take)/gather | solution.py:39
  280.2 30.7 %psum.31 = f32[]{:T(128)} all-reduce(f32[]{:T(128)} %get-tuple-element.11), channel_id=1, replica_groups=mesh['region'=2,'graph'=16] {'graph'}, use_global_device_ids=true, to_apply=%region_28.30 | all-reduce | flops 1 | bytes 8 | tf_op jit(solution)/shard_map/psum | solution.py:108
  (151 shorter events, 101.5 us)
Async XLA Ops:
  0.6 6.7 %copy-start = (bf16[8,5,128,128]{3,2,1,0:T(8,128)(2,1)S(1)}, bf16[8,5,128,128]{3,2,1,0:T(8,128)(2,1)}, u32[]{:S(2)}) copy-start(bf16[8,5,128,128]{3,2,1,0:T(8,128)(2,1)} %param.13) | copy-start | bytes 3932164
  4.1 16.9 %copy-start.1 = (f32[96,8,128]{2,1,0:T(8,128)S(1)}, f32[96,8,128]{2,1,0:T(8,128)}, u32[]{:S(2)}) copy-start(f32[96,8,128]{2,1,0:T(8,128)} %param.11) | copy-start | bytes 1179652
  4.1 48.7 %collective-permute-start.4 = (f32[96,4,128]{2,1,0:T(4,128)}, f32[96,4,128]{2,1,0:T(4,128)}, u32[]{:S(2)}, u32[]{:S(2)}) collective-permute-start(f32[96,4,128]{2,1,0:T(4,128)} %bitcast.18), channel_id=1, source_target_pairs={{0,1},{1,2},{2,3},{3,4},{4,5},{5,6},{6,7},{7,8},{8,9},{9,10},{10,1... | collective-permute-start | bytes 589832 | tf_op jit(solution)/shard_map/ppermute | solution.py:16
  9.4 31.0 %collective-permute-start = (f32[1,4,128]{2,1,0:T(4,128)}, f32[1,4,128]{2,1,0:T(4,128)}, u32[]{:S(2)}, u32[]{:S(2)}) collective-permute-start(f32[1,4,128]{2,1,0:T(4,128)} %get-tuple-element.49), channel_id=1, source_target_pairs={{1,0},{2,1},{3,2},{4,3},{5,4},{6,5},{7,6},{8,7},{9,8},{10,9},{11,1... | collective-permute-start | bytes 6152 | tf_op jit(solution)/shard_map/ppermute | solution.py:16
  10.7 31.7 %collective-permute-start.1 = (f32[1,4,128]{2,1,0:T(4,128)}, f32[1,4,128]{2,1,0:T(4,128)S(1)}, u32[]{:S(2)}, u32[]{:S(2)}) collective-permute-start(f32[1,4,128]{2,1,0:T(4,128)} %get-tuple-element.48), channel_id=1, source_target_pairs={{0,1},{1,2},{2,3},{3,4},{4,5},{5,6},{6,7},{7,8},{8,9},{9,10},{10,1... | collective-permute-start | bytes 6152 | tf_op jit(solution)/shard_map/ppermute | solution.py:16
  15.2 33.9 %collective-permute-start.2 = (f32[1,4,128]{2,1,0:T(4,128)}, f32[1,4,128]{2,1,0:T(4,128)S(1)}, u32[]{:S(2)}, u32[]{:S(2)}) collective-permute-start(f32[1,4,128]{2,1,0:T(4,128)} %get-tuple-element.47), channel_id=1, source_target_pairs={{2,0},{3,1},{4,2},{5,3},{6,4},{7,5},{8,6},{9,7},{10,8},{11,9},{12,... | collective-permute-start | bytes 6152 | tf_op jit(solution)/shard_map/ppermute | solution.py:16
  16.5 34.5 %collective-permute-start.3 = (f32[1,4,128]{2,1,0:T(4,128)}, f32[1,4,128]{2,1,0:T(4,128)S(1)}, u32[]{:S(2)}, u32[]{:S(2)}) collective-permute-start(f32[1,4,128]{2,1,0:T(4,128)} %get-tuple-element.46), channel_id=1, source_target_pairs={{0,2},{1,3},{2,4},{3,5},{4,6},{5,7},{6,8},{7,9},{8,10},{9,11},{10,... | collective-permute-start | bytes 6152 | tf_op jit(solution)/shard_map/ppermute | solution.py:16
  40.4 18.1 %collective-permute-start.5 = (f32[96,4,128]{2,1,0:T(4,128)}, f32[96,4,128]{2,1,0:T(4,128)S(1)}, u32[]{:S(2)}, u32[]{:S(2)}) collective-permute-start(f32[96,4,128]{2,1,0:T(4,128)} %bitcast.19), channel_id=1, source_target_pairs={{1,0},{2,1},{3,2},{4,3},{5,4},{6,5},{7,6},{8,7},{9,8},{10,9},{11,1... | collective-permute-start | bytes 589832 | tf_op jit(solution)/shard_map/ppermute | solution.py:16
  42.4 18.0 %collective-permute-start.6 = (f32[96,4,128]{2,1,0:T(4,128)}, f32[96,4,128]{2,1,0:T(4,128)S(1)}, u32[]{:S(2)}, u32[]{:S(2)}) collective-permute-start(f32[96,4,128]{2,1,0:T(4,128)} %bitcast.190), channel_id=1, source_target_pairs={{0,2},{1,3},{2,4},{3,5},{4,6},{5,7},{6,8},{7,9},{8,10},{9,11},{10,... | collective-permute-start | bytes 589832 | tf_op jit(solution)/shard_map/ppermute | solution.py:16
  49.0 18.5 %collective-permute-start.7 = (f32[96,4,128]{2,1,0:T(4,128)}, f32[96,4,128]{2,1,0:T(4,128)}, u32[]{:S(2)}, u32[]{:S(2)}) collective-permute-start(f32[96,4,128]{2,1,0:T(4,128)} %bitcast.189), channel_id=1, source_target_pairs={{2,0},{3,1},{4,2},{5,3},{6,4},{7,5},{8,6},{9,7},{10,8},{11,9},{12,... | collective-permute-start | bytes 589832 | tf_op jit(solution)/shard_map/ppermute | solution.py:16
  51.0 24.5 %collective-permute-start.8 = (f32[96,4,128]{2,0,1:T(8,128)}, f32[96,4,128]{2,0,1:T(8,128)}, u32[]{:S(2)}, u32[]{:S(2)}) collective-permute-start(f32[96,4,128]{2,0,1:T(8,128)} %get-tuple-element.29), channel_id=1, source_target_pairs={{1,0},{2,1},{3,2},{4,3},{5,4},{6,5},{7,6},{8,7},{9,8},{10,9},{11,1... | collective-permute-start | bytes 589832 | tf_op jit(solution)/shard_map/ppermute | solution.py:16
  52.9 24.2 %collective-permute-start.9 = (f32[96,4,128]{2,0,1:T(8,128)}, f32[96,4,128]{2,0,1:T(8,128)}, u32[]{:S(2)}, u32[]{:S(2)}) collective-permute-start(f32[96,4,128]{2,0,1:T(8,128)} %get-tuple-element.28), channel_id=1, source_target_pairs={{0,1},{1,2},{2,3},{3,4},{4,5},{5,6},{6,7},{7,8},{8,9},{9,10},{10,1... | collective-permute-start | bytes 589832 | tf_op jit(solution)/shard_map/ppermute | solution.py:16
  58.4 20.3 %collective-permute-start.10 = (f32[96,4,128]{2,0,1:T(8,128)}, f32[96,4,128]{2,0,1:T(8,128)}, u32[]{:S(2)}, u32[]{:S(2)}) collective-permute-start(f32[96,4,128]{2,0,1:T(8,128)} %get-tuple-element.27), channel_id=1, source_target_pairs={{2,0},{3,1},{4,2},{5,3},{6,4},{7,5},{8,6},{9,7},{10,8},{11,9},{12,... | collective-permute-start | bytes 589832 | tf_op jit(solution)/shard_map/ppermute | solution.py:16
  60.4 19.9 %collective-permute-start.11 = (f32[96,4,128]{2,0,1:T(8,128)S(1)}, f32[96,4,128]{2,0,1:T(8,128)}, u32[]{:S(2)}, u32[]{:S(2)}) collective-permute-start(f32[96,4,128]{2,0,1:T(8,128)S(1)} %get-tuple-element.26), channel_id=1, source_target_pairs={{0,2},{1,3},{2,4},{3,5},{4,6},{5,7},{6,8},{7,9},{8,10},{9,11},{10,... | collective-permute-start | bytes 589832 | tf_op jit(solution)/shard_map/ppermute | solution.py:16
  99.5 16.5 %collective-permute-start.12 = (f32[96,4,128]{2,0,1:T(8,128)}, f32[96,4,128]{2,0,1:T(8,128)}, u32[]{:S(2)}, u32[]{:S(2)}) collective-permute-start(f32[96,4,128]{2,0,1:T(8,128)} %bitcast.41), channel_id=1, source_target_pairs={{0,1},{1,2},{2,3},{3,4},{4,5},{5,6},{6,7},{7,8},{8,9},{9,10},{10,1... | collective-permute-start | bytes 589832 | tf_op jit(solution)/shard_map/ppermute | solution.py:16
  104.4 15.3 %collective-permute-start.13 = (f32[96,4,128]{2,0,1:T(8,128)}, f32[96,4,128]{2,0,1:T(8,128)}, u32[]{:S(2)}, u32[]{:S(2)}) collective-permute-start(f32[96,4,128]{2,0,1:T(8,128)} %bitcast.42), channel_id=1, source_target_pairs={{1,0},{2,1},{3,2},{4,3},{5,4},{6,5},{7,6},{8,7},{9,8},{10,9},{11,1... | collective-permute-start | bytes 589832 | tf_op jit(solution)/shard_map/ppermute | solution.py:16
  108.1 30.2 %collective-permute-start.16 = (f32[96,4,128]{2,0,1:T(8,128)}, f32[96,4,128]{2,0,1:T(8,128)}, u32[]{:S(2)}, u32[]{:S(2)}) collective-permute-start(f32[96,4,128]{2,0,1:T(8,128)} %get-tuple-element.25), channel_id=1, source_target_pairs={{1,0},{2,1},{3,2},{4,3},{5,4},{6,5},{7,6},{8,7},{9,8},{10,9},{11,1... | collective-permute-start | bytes 589832 | tf_op jit(solution)/shard_map/ppermute | solution.py:16
  109.4 15.5 %collective-permute-start.14 = (f32[96,4,128]{2,0,1:T(8,128)}, f32[96,4,128]{2,0,1:T(8,128)S(1)}, u32[]{:S(2)}, u32[]{:S(2)}) collective-permute-start(f32[96,4,128]{2,0,1:T(8,128)} %bitcast.188), channel_id=1, source_target_pairs={{0,2},{1,3},{2,4},{3,5},{4,6},{5,7},{6,8},{7,9},{8,10},{9,11},{10,... | collective-permute-start | bytes 589832 | tf_op jit(solution)/shard_map/ppermute | solution.py:16
  114.7 15.9 %collective-permute-start.15 = (f32[96,4,128]{2,0,1:T(8,128)}, f32[96,4,128]{2,0,1:T(8,128)S(1)}, u32[]{:S(2)}, u32[]{:S(2)}) collective-permute-start(f32[96,4,128]{2,0,1:T(8,128)} %bitcast.186), channel_id=1, source_target_pairs={{2,0},{3,1},{4,2},{5,3},{6,4},{7,5},{8,6},{9,7},{10,8},{11,9},{12,... | collective-permute-start | bytes 589832 | tf_op jit(solution)/shard_map/ppermute | solution.py:16
  116.0 24.7 %collective-permute-start.17 = (f32[96,4,128]{2,0,1:T(8,128)}, f32[96,4,128]{2,0,1:T(8,128)}, u32[]{:S(2)}, u32[]{:S(2)}) collective-permute-start(f32[96,4,128]{2,0,1:T(8,128)} %get-tuple-element.24), channel_id=1, source_target_pairs={{0,1},{1,2},{2,3},{3,4},{4,5},{5,6},{6,7},{7,8},{8,9},{9,10},{10,1... | collective-permute-start | bytes 589832 | tf_op jit(solution)/shard_map/ppermute | solution.py:16
  119.6 23.4 %collective-permute-start.18 = (f32[96,4,128]{2,0,1:T(8,128)}, f32[96,4,128]{2,0,1:T(8,128)}, u32[]{:S(2)}, u32[]{:S(2)}) collective-permute-start(f32[96,4,128]{2,0,1:T(8,128)} %get-tuple-element.23), channel_id=1, source_target_pairs={{2,0},{3,1},{4,2},{5,3},{6,4},{7,5},{8,6},{9,7},{10,8},{11,9},{12,... | collective-permute-start | bytes 589832 | tf_op jit(solution)/shard_map/ppermute | solution.py:16
  124.9 20.5 %collective-permute-start.19 = (f32[96,4,128]{2,0,1:T(8,128)S(1)}, f32[96,4,128]{2,0,1:T(8,128)}, u32[]{:S(2)}, u32[]{:S(2)}) collective-permute-start(f32[96,4,128]{2,0,1:T(8,128)S(1)} %get-tuple-element.22), channel_id=1, source_target_pairs={{0,2},{1,3},{2,4},{3,5},{4,6},{5,7},{6,8},{7,9},{8,10},{9,11},{10,... | collective-permute-start | bytes 589832 | tf_op jit(solution)/shard_map/ppermute | solution.py:16
  138.3 9.4 %copy-start.3 = (s32[96,8,128]{2,1,0:T(8,128)S(1)}, s32[96,8,128]{2,1,0:T(8,128)}, u32[]{:S(2)}) copy-start(s32[96,8,128]{2,1,0:T(8,128)} %param.10) | copy-start | bytes 1179652
  138.3 9.4 %copy-start.7 = (f32[95,8,128]{2,0,1:T(8,128)S(1)}, f32[95,8,128]{2,0,1:T(8,128)}, u32[]{:S(2)}) copy-start(f32[95,8,128]{2,0,1:T(8,128)} %get-tuple-element.38) | copy-start | bytes 1167364
  236.4 13.5 %collective-permute-start.20 = (f32[96,4,128]{2,0,1:T(8,128)}, f32[96,4,128]{2,0,1:T(8,128)}, u32[]{:S(2)}, u32[]{:S(2)}) collective-permute-start(f32[96,4,128]{2,0,1:T(8,128)} %bitcast.64), channel_id=1, source_target_pairs={{0,1},{1,2},{2,3},{3,4},{4,5},{5,6},{6,7},{7,8},{8,9},{9,10},{10,1... | collective-permute-start | bytes 589832 | tf_op jit(solution)/shard_map/ppermute | solution.py:16
  238.9 14.6 %collective-permute-start.21 = (f32[96,4,128]{2,0,1:T(8,128)S(1)}, f32[96,4,128]{2,0,1:T(8,128)}, u32[]{:S(2)}, u32[]{:S(2)}) collective-permute-start(f32[96,4,128]{2,0,1:T(8,128)S(1)} %bitcast.184), channel_id=1, source_target_pairs={{1,0},{2,1},{3,2},{4,3},{5,4},{6,5},{7,6},{8,7},{9,8},{10,9},{11,1... | collective-permute-start | bytes 589832 | tf_op jit(solution)/shard_map/ppermute | solution.py:16
  242.0 29.9 %collective-permute-start.24 = (f32[96,4,128]{2,0,1:T(8,128)}, f32[96,4,128]{2,0,1:T(8,128)}, u32[]{:S(2)}, u32[]{:S(2)}) collective-permute-start(f32[96,4,128]{2,0,1:T(8,128)} %get-tuple-element.21), channel_id=1, source_target_pairs={{1,0},{2,1},{3,2},{4,3},{5,4},{6,5},{7,6},{8,7},{9,8},{10,9},{11,1... | collective-permute-start | bytes 589832 | tf_op jit(solution)/shard_map/ppermute | solution.py:16
  243.3 14.9 %collective-permute-start.22 = (f32[96,4,128]{2,0,1:T(8,128)}, f32[96,4,128]{2,0,1:T(8,128)S(1)}, u32[]{:S(2)}, u32[]{:S(2)}) collective-permute-start(f32[96,4,128]{2,0,1:T(8,128)} %bitcast.187), channel_id=1, source_target_pairs={{0,2},{1,3},{2,4},{3,5},{4,6},{5,7},{6,8},{7,9},{8,10},{9,11},{10,... | collective-permute-start | bytes 589832 | tf_op jit(solution)/shard_map/ppermute | solution.py:16
  248.6 15.3 %collective-permute-start.23 = (f32[96,4,128]{2,0,1:T(8,128)S(1)}, f32[96,4,128]{2,0,1:T(8,128)S(1)}, u32[]{:S(2)}, u32[]{:S(2)}) collective-permute-start(f32[96,4,128]{2,0,1:T(8,128)S(1)} %bitcast.185), channel_id=1, source_target_pairs={{2,0},{3,1},{4,2},{5,3},{6,4},{7,5},{8,6},{9,7},{10,8},{11,9},{12,... | collective-permute-start | bytes 589832 | tf_op jit(solution)/shard_map/ppermute | solution.py:16
  249.9 23.6 %collective-permute-start.25 = (f32[96,4,128]{2,0,1:T(8,128)}, f32[96,4,128]{2,0,1:T(8,128)}, u32[]{:S(2)}, u32[]{:S(2)}) collective-permute-start(f32[96,4,128]{2,0,1:T(8,128)} %get-tuple-element.20), channel_id=1, source_target_pairs={{0,1},{1,2},{2,3},{3,4},{4,5},{5,6},{6,7},{7,8},{8,9},{9,10},{10,1... | collective-permute-start | bytes 589832 | tf_op jit(solution)/shard_map/ppermute | solution.py:16
  253.5 21.6 %collective-permute-start.26 = (f32[96,4,128]{2,0,1:T(8,128)}, f32[96,4,128]{2,0,1:T(8,128)}, u32[]{:S(2)}, u32[]{:S(2)}) collective-permute-start(f32[96,4,128]{2,0,1:T(8,128)} %get-tuple-element.19), channel_id=1, source_target_pairs={{2,0},{3,1},{4,2},{5,3},{6,4},{7,5},{8,6},{9,7},{10,8},{11,9},{12,... | collective-permute-start | bytes 589832 | tf_op jit(solution)/shard_map/ppermute | solution.py:16
  258.2 18.5 %collective-permute-start.27 = (f32[96,4,128]{2,0,1:T(8,128)S(1)}, f32[96,4,128]{2,0,1:T(8,128)}, u32[]{:S(2)}, u32[]{:S(2)}) collective-permute-start(f32[96,4,128]{2,0,1:T(8,128)S(1)} %get-tuple-element.18), channel_id=1, source_target_pairs={{0,2},{1,3},{2,4},{3,5},{4,6},{5,7},{6,8},{7,9},{8,10},{9,11},{10,... | collective-permute-start | bytes 589832 | tf_op jit(solution)/shard_map/ppermute | solution.py:16
  (7 other events, 37.3 us)
where the time goes:
time: 317 us; the launch traced here: 314 us
  blocking collectives  93.5 us (29%)
  starting transfers between devices  78.5 us (25%)
  other arithmetic  60.8 us (19%)
  local copies, waits for them, and re-layouts  53.7 us (17%)
  matrix products  18.2 us (6%)
  between operations  5.28 us (2%)
  waiting for transfers between devices  4.26 us (1%)
    ppermute x28, starting transfers between devices, shifted(): return lax.ppermute(block, axis, route)  78.5 us
    psum x2, blocking collectives, squares_sum(): return lax.psum(jnp.sum(residual * residual), 'graph')  62.8 us
    psum x1, blocking collectives, per_device(): step_size = norm_now / lax.psum(jnp.sum(direction * image), 'graph')  30.7 us
    scatter-add x16, other arithmetic, transpose_finish(): total = total.at[:, send_list[index]].add(arrived[-offset])  24.8 us
    scatter-add x4, other arithmetic, transpose_collect(): return blank.at[:, column_ids].add(terms)  21.3 us
    unnamed x36, local copies, waits for them, and re-layouts  16.3 us
    gather x12, local copies, waits for them, and re-layouts, forward_parcels(): field[:, send_list[index]]  16.1 us
    dot_general x7, matrix products, block_product(): jnp.einsum(form, weights, lower, preferred_element_type=jnp.float32)  10.4 us
  transfers between devices with their start and end apart: 28, of which 2 were waited for; matrix products, arithmetic and copies ran while one was open for 25% of the time, Pallas kernels for 0%

commit v1 on v0

v1 whole, which is shorter than its diff:
```python
import functools

import jax
import jax.numpy as jnp
from jax import lax
from jax.experimental import pallas as pl
from jax.experimental.pallas import tpu as pltpu
from jax.sharding import PartitionSpec as P

ITERS = 2
APPLIED = ITERS + 1
OFFSETS = (1, -1, 2, -2)
time_tie = 0.5
CHUNKS = 2
MESH = pl.DeviceIdType.MESH
OWN, PAIR, FACE, FAR, SIDE = range(5)


def shifted(block, axis, distance):
    devices = range(lax.axis_size(axis))
    route = [(i - distance, i) for i in devices if i - distance in devices]
    return lax.ppermute(block, axis, route)


def split_parts(field):
    upper = field.astype(jnp.bfloat16)
    lower = (field - upper.astype(jnp.float32)).astype(jnp.bfloat16)
    return [upper, lower]


def fold_rows(values):
    total = values[0:8]
    for start in range(8, values.shape[0], 8):
        total = total + values[start : start + 8]
    return total


def total_of(tile):
    return jnp.sum(jnp.sum(tile, axis=0, keepdims=True), axis=1, keepdims=True)


def cg_kernel(
    count,
    blocks,
    slots,
    steps,
    places_ref,
    before_ref,
    last_ref,
    observed_ref,
    mask_ref,
    guess_ref,
    prior_ref,
    weights_ref,
    solution_ref,
    residual_ref,
    *scratch,
):
    ext = [scratch[s * CHUNKS : (s + 1) * CHUNKS] for s in range(APPLIED)]
    final, mask_f, right, sums, kept, out_terms, in_terms, diag, red_out, red_in = scratch[APPLIED * CHUNKS : -4]
    send_sem, recv_sem, red_send_sem, red_recv_sem = scratch[-4:]
    width = guess_ref.shape[2]
    me = lax.axis_index("graph")
    core = lax.rem(me, 2)
    face = lax.rem(me // 2, 2)
    pair_id = me + 1 - 2 * core
    face_id = me + 2 - 4 * face
    far_src = me - 4 + 8 * face
    far_dst = me + 4 - 8 * face
    has_src = (far_src >= 0) & (far_src < count)
    has_dst = (far_dst >= 0) & (far_dst < count)
    same = core == face
    always = me >= 0
    part = steps // CHUNKS
    terms = blocks * slots
    f32 = jnp.float32

    barrier = pltpu.get_barrier_semaphore()
    for step in range(1, count):
        pl.semaphore_signal(barrier, inc=1, device_id={"graph": lax.rem(me + step, count)}, device_id_type=MESH)

    for i in range(blocks):
        for chunk in range(CHUNKS):
            ext[0][chunk][i] = guess_ref[chunk * part : (chunk + 1) * part, i, :]

    @pl.when(jnp.logical_not(has_src))
    def _():
        for held in scratch[: APPLIED * CHUNKS]:
            held[FAR * blocks : (FAR + 1) * blocks] = jnp.zeros((blocks, part, width), f32)

    @pl.when(same & jnp.logical_not(has_src))
    def _():
        for held in scratch[: APPLIED * CHUNKS]:
            held[SIDE * blocks : (SIDE + 1) * blocks] = jnp.zeros((blocks, part, width), f32)

    sums[terms] = jnp.zeros(sums.shape[1:], f32)
    pl.semaphore_wait(barrier, count - 1)

    pending = []

    def field_copy(s, chunk, kind, src_role, dst_role, target):
        return pltpu.make_async_remote_copy(
            src_ref=ext[s][chunk].at[pl.ds(src_role * blocks, blocks)],
            dst_ref=ext[s][chunk].at[pl.ds(dst_role * blocks, blocks)],
            send_sem=send_sem.at[s, chunk, kind],
            recv_sem=recv_sem.at[s, chunk, kind],
            device_id={"graph": target},
            device_id_type=MESH,
        )

    def term_rows(s, chunk):
        if s == 0 and chunk == 0:
            return 0, part + 8
        return 8 + chunk * part, part

    def term_copy(s, chunk, role, target):
        start, size = term_rows(s, chunk)
        return pltpu.make_async_remote_copy(
            src_ref=out_terms.at[s, pl.ds((role - 1) * blocks, blocks), pl.ds(start, size)],
            dst_ref=in_terms.at[s, pl.ds((role - 1) * blocks, blocks), pl.ds(start, size)],
            send_sem=send_sem.at[s, chunk, 3 + role],
            recv_sem=recv_sem.at[s, chunk, 3 + role],
            device_id={"graph": target},
            device_id_type=MESH,
        )

    def start(cond, make):
        copy = make()
        pl.when(cond)(copy.start)
        pending.append((cond, copy))

    def arrived(cond, make):
        pl.when(cond)(make().wait_recv)

    def copies(s, chunk):
        field = {
            PAIR: lambda: field_copy(s, chunk, 0, OWN, PAIR, pair_id),
            FACE: lambda: field_copy(s, chunk, 1, OWN, FACE, face_id),
            FAR: lambda: field_copy(s, chunk, 2, FACE, FAR, far_dst),
            SIDE: lambda: field_copy(s, chunk, 3, FACE, SIDE, pair_id),
            "other": lambda: field_copy(s, chunk, 3, FAR, SIDE, pair_id),
        }
        term = {
            PAIR: lambda: term_copy(s, chunk, PAIR, pair_id),
            FACE: lambda: term_copy(s, chunk, FACE, face_id),
            FAR: lambda: term_copy(s, chunk, FAR, far_src),
            SIDE: lambda: term_copy(s, chunk, SIDE, pair_id),
        }
        return field, term

    def add_terms(s, chunk, role, other):
        start_row, size = term_rows(s, chunk)
        rows = pl.ds(start_row, size)

        def body(j, carry):
            at = (role - 1) * blocks + j
            out_terms[s, at, rows] = out_terms[s, at, rows] + in_terms[s, (other - 1) * blocks + j, rows]
            return carry

        lax.fori_loop(0, blocks, body, 0)

    def send_stage(s, chunk):
        field, term = copies(s, chunk)
        start(always, field[FACE])
        start(always, field[PAIR])
        start_row, size = term_rows(s, chunk)
        with_ones = size > part
        rows = pl.ds(start_row, size)

        def row_body(i, carry):
            own = ext[s][chunk][i]
            pieces = split_parts(own)
            if with_ones:
                pieces.append(jnp.ones((16, own.shape[1]), jnp.bfloat16))
            stacked = jnp.concatenate(pieces, axis=0)
            for k in range(slots):
                made = jnp.dot(stacked, weights_ref[i, k], preferred_element_type=f32)
                term_now = made[:part] + made[part : 2 * part]
                if with_ones:
                    term_now = jnp.concatenate([made[2 * part : 2 * part + 8], term_now], axis=0)
                at = i * slots + k
                sums[at, :size] = term_now + sums[before_ref[at], :size]
            return carry

        lax.fori_loop(0, blocks, row_body, 0)
        for role in (SIDE, FAR, PAIR, FACE):

            def pick(j, carry, role=role):
                out_terms[s, (role - 1) * blocks + j, rows] = sums[last_ref[role * blocks + j], :size]
                return carry

            lax.fori_loop(0, blocks, pick, 0)
            if role == SIDE:
                start(jnp.logical_not(same) | has_src, term[SIDE])
            if role == FAR:
                start(same & has_src, term[FAR])
            if role == PAIR:
                start(always, term[PAIR])

        def keep(j, carry):
            kept[s, j, rows] = sums[last_ref[j], :size]
            return carry

        lax.fori_loop(0, blocks, keep, 0)

    def far_terms_stage(s, chunk):
        field, term = copies(s, chunk)
        moved = jnp.logical_not(same) & has_src
        arrived(same | has_src, term[SIDE])

        @pl.when(moved)
        def _():
            add_terms(s, chunk, FAR, SIDE)

        start(moved, term[FAR])

    def face_relay_stage(s, chunk):
        field, term = copies(s, chunk)
        arrived(always, field[FACE])
        start(has_dst, field[FAR])
        start(same, field[SIDE])

    def face_terms_stage(s, chunk):
        field, term = copies(s, chunk)

        @pl.when(same)
        def _():
            add_terms(s, chunk, FACE, SIDE)

        arrived(has_dst, term[FAR])

        @pl.when(has_dst)
        def _():
            add_terms(s, chunk, FACE, FAR)

        start(always, term[FACE])

    def far_relay_stage(s, chunk):
        field, term = copies(s, chunk)
        arrived(has_src, field[FAR])
        start(jnp.logical_not(same) & has_src, field["other"])

    def finish_stage(s, chunk):
        field, term = copies(s, chunk)
        start_row, size = term_rows(s, chunk)
        with_ones = size > part
        here = pl.ds(chunk * part, part)
        arrived(always, field[PAIR])
        arrived(jnp.logical_not(same) | has_src, field[SIDE])
        arrived(always, term[PAIR])
        arrived(always, term[FACE])

        def row_body(i, carry):
            made = None
            for k in range(slots):
                pieces = split_parts(ext[s][chunk][places_ref[i * slots + k]])
                if with_ones:
                    pieces.append(jnp.ones((16, width), jnp.bfloat16))
                stacked = jnp.concatenate(pieces, axis=0)
                product = lax.dot_general(
                    stacked, weights_ref[i, k], (((1,), (1,)), ((), ())), preferred_element_type=f32
                )
                made = product if made is None else made + product
            trows = pl.ds(start_row, size)
            returned = (
                kept[s, i, trows]
                + in_terms[s, (PAIR - 1) * blocks + i, trows]
                + in_terms[s, (FACE - 1) * blocks + i, trows]
            )
            if with_ones:
                diag[i] = made[2 * part : 2 * part + 8] + returned[:8] + prior_ref[pl.ds(i, 1), :]
                returned = returned[8:]
            coupled = made[:part] + made[part : 2 * part] + returned
            now = ext[s][chunk][i]
            if chunk == 0:
                earlier = jnp.concatenate([now[:1], now[:-1]], axis=0)
            else:
                earlier = jnp.concatenate([ext[s][chunk - 1][i, part - 1 : part], now[:-1]], axis=0)
            if chunk == CHUNKS - 1:
                later = jnp.concatenate([now[1:], now[-1:]], axis=0)
            else:
                later = jnp.concatenate([now[1:], ext[s][chunk + 1][i, 0:1]], axis=0)
            diagonal = mask_f[i, here, :] + diag[i][:1]
            image = diagonal * now - coupled + time_tie * (2.0 * now - earlier - later)
            if s == 0:
                ext[1][chunk][i] = right[i, here, :] - image
            elif s == 1:
                ext[2][chunk][i] = image
                return (carry[0] + fold_rows(now * now), carry[1] + fold_rows(now * image))
            else:
                final[i, here, :] = image
            return carry

        zero = jnp.zeros((8, width), f32)
        return lax.fori_loop(0, blocks, row_body, (zero, zero))

    def reduce_start(index, tiles):
        for n, tile in enumerate(tiles):
            red_out[index, n] = tile
        sent = []
        for step in range(1, count):
            copy = pltpu.make_async_remote_copy(
                src_ref=red_out.at[index],
                dst_ref=red_in.at[index, step - 1],
                send_sem=red_send_sem.at[index],
                recv_sem=red_recv_sem.at[index],
                device_id={"graph": lax.rem(me + step, count)},
                device_id_type=MESH,
            )
            copy.start()

    def reduce_done(index, used):
        pltpu.make_async_copy(red_in.at[index], red_in.at[index], red_recv_sem.at[index]).wait()
        pltpu.make_async_copy(red_in.at[index], red_in.at[index], red_send_sem.at[index]).wait()
        values = []
        for n in range(used):
            tile = red_out[index, n]
            for step in range(1, count):
                tile = tile + red_in[index, step - 1, n]
            values.append(total_of(tile))
        return values

    def relay(s, chunk):
        far_terms_stage(s, chunk)
        face_relay_stage(s, chunk)
        face_terms_stage(s, chunk)
        far_relay_stage(s, chunk)

    zero = jnp.zeros((8, width), f32)
    dots = [zero, zero]
    for chunk in range(CHUNKS):
        send_stage(0, chunk)
    for i in range(blocks):
        seen = mask_ref[:, i, :].astype(f32)
        mask_f[i] = seen
        right[i] = seen * observed_ref[:, i, :]
    for s in range(APPLIED):
        for chunk in range(CHUNKS):
            relay(s, chunk)
            made = finish_stage(s, chunk)
            if s == 1:
                dots = [dots[0] + made[0], dots[1] + made[1]]
            if s + 1 < APPLIED:
                send_stage(s + 1, chunk)
        if s == 1:
            reduce_start(0, dots)
            norm_first, energy = reduce_done(0, 2)
            step_first = norm_first / energy

            def next_residual(i, carry):
                for chunk in range(CHUNKS):
                    fresh = ext[1][chunk][i] - step_first * ext[2][chunk][i]
                    right[i, pl.ds(chunk * part, part)] = fresh
                    carry = carry + fold_rows(fresh * fresh)
                return carry

            reduce_start(1, [lax.fori_loop(0, blocks, next_residual, zero)])
            (norm_second,) = reduce_done(1, 1)
            ratio = norm_second / norm_first

    def last_dot(i, carry):
        for chunk in range(CHUNKS):
            here = pl.ds(chunk * part, part)
            image = (1.0 + ratio) * ext[2][chunk][i] - step_first * final[i, here]
            direction = right[i, here] + ratio * ext[1][chunk][i]
            final[i, here] = image
            carry = carry + fold_rows(direction * image)
        return carry

    reduce_start(2, [lax.fori_loop(0, blocks, last_dot, zero)])
    (energy_second,) = reduce_done(2, 1)
    step_second = norm_second / energy_second
    for i in range(blocks):
        for chunk in range(CHUNKS):
            here = slice(chunk * part, (chunk + 1) * part)
            first = ext[1][chunk][i]
            fresh = right[i, here]
            direction = fresh + ratio * first
            solution_ref[here, i, :] = (ext[0][chunk][i] + step_first * first) + step_second * direction
            residual_ref[here, i, :] = fresh - step_second * final[i, here]
    for cond, copy in pending:
        pl.when(cond)(copy.wait_send)


def index_tables(block_cols, send_list, blocks):
    me = lax.axis_index("graph")
    core, face = me % 2, (me // 2) % 2
    listed = jnp.stack([shifted(send_list[index], "graph", offset) for index, offset in enumerate(OFFSETS)])
    role = jnp.stack(
        [
            jnp.where(core == 1, PAIR, SIDE),
            jnp.where(core == 0, PAIR, SIDE),
            jnp.where(face == 1, FACE, FAR),
            jnp.where(face == 0, FACE, FAR),
        ]
    )
    received = (role[:, None] * blocks + listed).reshape(-1)
    table = jnp.concatenate([jnp.arange(blocks, dtype=jnp.int32), received.astype(jnp.int32)])
    flat = block_cols.reshape(-1)
    places = jnp.sum(jnp.where(flat[:, None] == jnp.arange(table.shape[0])[None], table[None], 0), axis=1)
    terms = flat.shape[0]
    order = jnp.arange(terms)
    match = (places[None, :] == places[:, None]) & (order[None, :] < order[:, None])
    before = jnp.max(jnp.where(match, order[None, :], -1), axis=1)
    hits = places[None, :] == jnp.arange(5 * blocks)[:, None]
    last = jnp.max(jnp.where(hits, order[None, :], -1), axis=1)
    before = jnp.where(before < 0, terms, before)
    last = jnp.where(last < 0, terms, last)
    return places.astype(jnp.int32), before.astype(jnp.int32), last.astype(jnp.int32)


def per_device(count, observed, mask, first_guess, diag_weight, coupling, block_cols, send_rows):
    steps, blocks, width = observed.shape
    slots = coupling.shape[1]
    terms = blocks * slots
    part = steps // CHUNKS
    places, before, last = index_tables(block_cols, send_rows[0], blocks)
    f32 = jnp.float32
    vmem = pl.BlockSpec(memory_space=pltpu.VMEM)
    smem = pl.BlockSpec(memory_space=pltpu.SMEM)
    shape = jax.ShapeDtypeStruct((steps, blocks, width), f32)
    return pl.pallas_call(
        functools.partial(cg_kernel, count, blocks, slots, steps),
        out_shape=(shape, shape),
        in_specs=[smem] * 3 + [vmem] * 5,
        out_specs=(vmem, vmem),
        scratch_shapes=[pltpu.VMEM((5 * blocks, part, width), f32)] * (APPLIED * CHUNKS)
        + [
            pltpu.VMEM((blocks, steps, width), f32),
            pltpu.VMEM((blocks, steps, width), f32),
            pltpu.VMEM((blocks, steps, width), f32),
            pltpu.VMEM((terms + 1, part + 8, width), f32),
            pltpu.VMEM((APPLIED, blocks, steps + 8, width), f32),
            pltpu.VMEM((APPLIED, 4 * blocks, steps + 8, width), f32),
            pltpu.VMEM((APPLIED, 4 * blocks, steps + 8, width), f32),
            pltpu.VMEM((blocks, 8, width), f32),
            pltpu.VMEM((3, 2, 8, width), f32),
            pltpu.VMEM((3, count - 1, 2, 8, width), f32),
            pltpu.SemaphoreType.DMA((APPLIED, CHUNKS, 8)),
            pltpu.SemaphoreType.DMA((APPLIED, CHUNKS, 8)),
            pltpu.SemaphoreType.DMA((3,)),
            pltpu.SemaphoreType.DMA((3,)),
        ],
        compiler_params=pltpu.CompilerParams(
            collective_id=0, has_side_effects=True, vmem_limit_bytes=48 * 1024 * 1024
        ),
    )(places, before, last, observed, mask, first_guess, diag_weight, coupling)


def solution(mesh):
    fields = P(None, ("region", "graph"), None)
    placed = (
        fields,
        fields,
        fields,
        P(("region", "graph"), None),
        P(("region", "graph"), None, None, None),
        P(("region", "graph"), None),
        P(("region", "graph"), None, None),
    )
    return jax.shard_map(
        functools.partial(per_device, mesh.shape["graph"]),
        mesh=mesh,
        in_specs=placed,
        out_specs=(fields, fields),
        check_vma=False,
    )
```

time: 317 us -> 123 us (0.39)
  Pallas kernels: 0 us -> 101 us
  blocking collectives: 93.5 us -> 0 us
  starting transfers between devices: 78.5 us -> 12.3 us
  other arithmetic: 60.8 us -> 0.5 us
  local copies, waits for them, and re-layouts: 53.7 us -> 8.17 us
  matrix products: 18.2 us -> 0 us
  between operations: 5.28 us -> 0.76 us
  waiting for transfers between devices: 4.26 us -> 0.37 us
    pallas_call x0 -> x1, Pallas kernels: none -> 101 us  [per_device(): pl.pallas_call(functools.partial(cg_kernel, count, blocks, slots, steps),...]
    psum x3 -> x0, blocking collectives: 93.5 us -> none  [the longest x2 62.8 us: squares_sum(): return lax.psum(jnp.sum(residual * residual), 'graph')]
    ppermute x28 -> x4, starting transfers between devices: 78.5 us -> 12.3 us  [shifted(): return lax.ppermute(block, axis, route)]
    scatter-add x20 -> x0, other arithmetic: 46.1 us -> none  [the longest x16 24.8 us: transpose_finish(): total = total.at[:, send_list[index]].add(arrived[-offset])]
    gather x15 -> x0, local copies, waits for them, and re-layouts: 25.8 us -> none  [the longest x12 16.1 us: forward_parcels(): field[:, send_list[index]]]
    dot_general x14 -> x0, matrix products: 18.2 us -> none  [the longest x7 10.4 us: block_product(): jnp.einsum(form, weights, lower, preferred_element_type=jnp.float32)]
    unnamed x36 -> x12, local copies, waits for them, and re-layouts: 16.3 us -> 6.48 us
    slice x10 -> x0, local copies, waits for them, and re-layouts: 7.03 us -> none  [the longest x4 4.36 us: transpose_parcels(): parcels[-offset] = collected[:, start:start + capacity]]
  transfers between devices with their start and end apart: 28 -> 4, of which waited for: 2 -> 1; matrix products, arithmetic and copies ran while one was open for 25% -> 1% of each run, Pallas kernels for 0% -> 0%
where the time goes in v1:
time: 123 us
  Pallas kernels  101 us (82%)
  starting transfers between devices  12.3 us (10%)
  local copies, waits for them, and re-layouts  8.17 us (7%)
    pallas_call x1, Pallas kernels, per_device(): pl.pallas_call(functools.partial(cg_kernel, count, blocks, slots, steps),...  101 us
    ppermute x4, starting transfers between devices, shifted(): return lax.ppermute(block, axis, route)  12.3 us
    unnamed x12, local copies, waits for them, and re-layouts  6.48 us
  transfers between devices with their start and end apart: 4, of which 1 were waited for; matrix products, arithmetic and copies ran while one was open for 1% of the time, Pallas kernels for 0%

profile of v1, /device:TPU:0, one launch (start us, length us, event | category | flops | bytes accessed | tf_op | source)
XLA Modules:
  0.0 122.7 jit_solution(12887135985444768516)
XLA Ops:
  0.6 0.8 slice_bitcast_fusion.3
  1.5 2.3 %collective-permute-start = (s32[4]{0:T(128)S(1)}, s32[4]{0:T(128)S(1)}, u32[]{:S(2)}, u32[]{:S(2)}) collective-permute-start(s32[4]{0:T(128)S(1)} %get-tuple-element.4), channel_id=1, source_target_pairs={{0,1},{1,2},{2,3},{3,4},{4,5},{5,6},{6,7},{7,8},{8,9},{9,10},{10,1... | collective-permute-start | bytes 56 | tf_op jit(solution)/shard_map/ppermute | solution.py:22
  3.8 1.3 %collective-permute-start.1 = (s32[4]{0:T(128)S(1)}, s32[4]{0:T(128)S(1)}, u32[]{:S(2)}, u32[]{:S(2)}) collective-permute-start(s32[4]{0:T(128)S(1)} %get-tuple-element.5), channel_id=1, source_target_pairs={{1,0},{2,1},{3,2},{4,3},{5,4},{6,5},{7,6},{8,7},{9,8},{10,9},{11,1... | collective-permute-start | bytes 56 | tf_op jit(solution)/shard_map/ppermute | solution.py:22
  5.1 1.3 %collective-permute-start.3 = (s32[4]{0:T(128)S(1)}, s32[4]{0:T(128)S(1)}, u32[]{:S(2)}, u32[]{:S(2)}) collective-permute-start(s32[4]{0:T(128)S(1)} %get-tuple-element.6), channel_id=1, source_target_pairs={{2,0},{3,1},{4,2},{5,3},{6,4},{7,5},{8,6},{9,7},{10,8},{11,9},{12,... | collective-permute-start | bytes 56 | tf_op jit(solution)/shard_map/ppermute | solution.py:22
  6.4 7.4 %collective-permute-start.2 = (s32[4]{0:T(128)S(1)}, s32[4]{0:T(128)S(1)}, u32[]{:S(2)}, u32[]{:S(2)}) collective-permute-start(s32[4]{0:T(128)S(1)} %get-tuple-element.7), channel_id=1, source_target_pairs={{0,2},{1,3},{2,4},{3,5},{4,6},{5,7},{6,8},{7,9},{8,10},{9,11},{10,... | collective-permute-start | bytes 56 | tf_op jit(solution)/shard_map/ppermute | solution.py:22
  13.9 0.8 eq.52
  14.7 0.1 add_multiply_fusion
  14.7 0.0 collective-permute-done
  14.7 0.0 collective-permute-done.1
  14.7 0.0 collective-permute-done.3
  14.8 0.4 collective-permute-done.2
  15.1 0.1 add_add_fusion
  15.2 0.1 add.24
  15.3 0.1 pad_add_fusion
  15.4 0.1 select_reduce_fusion.2.places_ref
  15.4 0.2 select_reduce_fusion
  15.6 0.0 copy-start
  15.7 1.3 %copy-done = bf16[8,5,128,128]{3,2,1,0:T(8,128)(2,1)S(1)} copy-done((bf16[8,5,128,128]{3,2,1,0:T(8,128)(2,1)S(1)}, bf16[8,5,128,128]{3,2,1,0:T(8,128)(2,1)}, u32[]{:S(2)}) %copy-start) | copy-done | bytes 1310744
  17.0 0.0 copy-start.1
  17.0 1.0 copy-done.1
  18.0 0.0 copy-start.2
  18.0 1.0 copy-done.2
  19.0 0.0 copy-start.3
  19.0 1.0 copy-done.3
  20.0 0.0 copy-start.4
  20.0 0.7 copy-done.4
  20.6 100.5 %shard_map.86 = (f32[96,8,128]{2,1,0:T(8,128)S(1)}, f32[96,8,128]{2,1,0:T(8,128)S(1)}) custom-call(s32[40]{0:T(128)S(1)} %select_reduce_fusion.2.places_ref, s32[40]{0:T(128)S(1)} %get-tuple-element.9.before_ref, s32[40]{0:T(128)S(1)} %get-tuple-element.8.last_ref, f32[96,8,128]{2,1,0:T(8,128)S(1)} %copy-done.1, s32[96,8,128]{2,1,0:T(8,128)S(1)} %copy-done.2, ...), custom_call_target="tpu_custom_call" | custom-call | tf_op jit(solution)/shard_map/pallas_call | solution.py:422
  121.2 0.7 copy.11
  121.9 0.7 copy.12
  (2 shorter events, 0.0 us)
Async XLA Ops:
  1.5 13.3 %collective-permute-start = (s32[4]{0:T(128)S(1)}, s32[4]{0:T(128)S(1)}, u32[]{:S(2)}, u32[]{:S(2)}) collective-permute-start(s32[4]{0:T(128)S(1)} %get-tuple-element.4), channel_id=1, source_target_pairs={{0,1},{1,2},{2,3},{3,4},{4,5},{5,6},{6,7},{7,8},{8,9},{9,10},{10,1... | collective-permute-start | bytes 56 | tf_op jit(solution)/shard_map/ppermute | solution.py:22
  3.8 10.9 %collective-permute-start.1 = (s32[4]{0:T(128)S(1)}, s32[4]{0:T(128)S(1)}, u32[]{:S(2)}, u32[]{:S(2)}) collective-permute-start(s32[4]{0:T(128)S(1)} %get-tuple-element.5), channel_id=1, source_target_pairs={{1,0},{2,1},{3,2},{4,3},{5,4},{6,5},{7,6},{8,7},{9,8},{10,9},{11,1... | collective-permute-start | bytes 56 | tf_op jit(solution)/shard_map/ppermute | solution.py:22
  5.1 9.6 %collective-permute-start.3 = (s32[4]{0:T(128)S(1)}, s32[4]{0:T(128)S(1)}, u32[]{:S(2)}, u32[]{:S(2)}) collective-permute-start(s32[4]{0:T(128)S(1)} %get-tuple-element.6), channel_id=1, source_target_pairs={{2,0},{3,1},{4,2},{5,3},{6,4},{7,5},{8,6},{9,7},{10,8},{11,9},{12,... | collective-permute-start | bytes 56 | tf_op jit(solution)/shard_map/ppermute | solution.py:22
  6.4 8.7 %collective-permute-start.2 = (s32[4]{0:T(128)S(1)}, s32[4]{0:T(128)S(1)}, u32[]{:S(2)}, u32[]{:S(2)}) collective-permute-start(s32[4]{0:T(128)S(1)} %get-tuple-element.7), channel_id=1, source_target_pairs={{0,2},{1,3},{2,4},{3,5},{4,6},{5,7},{6,8},{7,9},{8,10},{9,11},{10,... | collective-permute-start | bytes 56 | tf_op jit(solution)/shard_map/ppermute | solution.py:22
  15.6 1.3 %copy-start = (bf16[8,5,128,128]{3,2,1,0:T(8,128)(2,1)S(1)}, bf16[8,5,128,128]{3,2,1,0:T(8,128)(2,1)}, u32[]{:S(2)}) copy-start(bf16[8,5,128,128]{3,2,1,0:T(8,128)(2,1)} %weights_ref.1) | copy-start | bytes 3932164
  17.0 1.0 copy-start.1
  18.0 1.0 copy-start.2
  19.0 1.0 copy-start.3
  20.0 0.7 copy-start.4

commit v2 on v1

--- a/solution.py
+++ b/solution.py
@@ -12,14 +12,9 @@
 OFFSETS = (1, -1, 2, -2)
 time_tie = 0.5
 CHUNKS = 2
+UNROLL = 4
 MESH = pl.DeviceIdType.MESH
 OWN, PAIR, FACE, FAR, SIDE = range(5)
-
-
-def shifted(block, axis, distance):
-    devices = range(lax.axis_size(axis))
-    route = [(i - distance, i) for i in devices if i - distance in devices]
-    return lax.ppermute(block, axis, route)
 
 
 def split_parts(field):
@@ -44,22 +39,29 @@
     blocks,
     slots,
     steps,
-    places_ref,
     before_ref,
-    last_ref,
-    observed_ref,
-    mask_ref,
-    guess_ref,
-    prior_ref,
-    weights_ref,
+    slot_last_ref,
+    cols_ref,
+    observed_hbm,
+    mask_hbm,
+    guess_hbm,
+    prior_hbm,
+    weights_hbm,
+    lists_hbm,
     solution_ref,
     residual_ref,
     *scratch,
 ):
     ext = [scratch[s * CHUNKS : (s + 1) * CHUNKS] for s in range(APPLIED)]
-    final, mask_f, right, sums, kept, out_terms, in_terms, diag, red_out, red_in = scratch[APPLIED * CHUNKS : -4]
-    send_sem, recv_sem, red_send_sem, red_recv_sem = scratch[-4:]
+    final, mask_f, right, sums, kept, out_terms, in_terms, diag, red_out, red_in = scratch[APPLIED * CHUNKS : -14]
+    observed_ref, mask_ref, guess_ref, prior_ref, weights_ref, lists_in, lists_ref, table_ref, last_ref = scratch[-14:-5]
+    send_sem, recv_sem, red_send_sem, red_recv_sem, load_sem = scratch[-5:]
     width = guess_ref.shape[2]
+    places = (guess_hbm, guess_ref), (weights_hbm, weights_ref), (mask_hbm, mask_ref)
+    places += (observed_hbm, observed_ref), (prior_hbm, prior_ref)
+    loads = [pltpu.make_async_copy(far, near, load_sem.at[n]) for n, (far, near) in enumerate(places)]
+    for load in loads:
+        load.start()
     me = lax.axis_index("graph")
     core = lax.rem(me, 2)
     face = lax.rem(me // 2, 2)
@@ -79,6 +81,7 @@
     for step in range(1, count):
         pl.semaphore_signal(barrier, inc=1, device_id={"graph": lax.rem(me + step, count)}, device_id_type=MESH)
 
+    loads[0].wait()
     for i in range(blocks):
         for chunk in range(CHUNKS):
             ext[0][chunk][i] = guess_ref[chunk * part : (chunk + 1) * part, i, :]
@@ -93,10 +96,62 @@
         for held in scratch[: APPLIED * CHUNKS]:
             held[SIDE * blocks : (SIDE + 1) * blocks] = jnp.zeros((blocks, part, width), f32)
 
+    capacity = lists_in.shape[3]
+    list_copies = []
+    for index, offset in enumerate(OFFSETS):
+        source, target = me - offset, me + offset
+        list_copies.append(
+            (
+                (source >= 0) & (source < count),
+                (target >= 0) & (target < count),
+                pltpu.make_async_remote_copy(
+                    src_ref=lists_hbm,
+                    dst_ref=lists_in.at[index],
+                    send_sem=load_sem.at[6 + index],
+                    recv_sem=load_sem.at[10 + index],
+                    device_id={"graph": target},
+                    device_id_type=MESH,
+                ),
+            )
+        )
+
+        @pl.when((source < 0) | (source >= count))
+        def _(index=index):
+            lists_in[index] = jnp.zeros(lists_in.shape[1:], jnp.int32)
+
     sums[terms] = jnp.zeros(sums.shape[1:], f32)
     pl.semaphore_wait(barrier, count - 1)
 
     pending = []
+    for _, wanted, copy in list_copies:
+        pl.when(wanted)(copy.start)
+        pending.append((wanted, copy))
+
+    def make_tables():
+        for wanted, _, copy in list_copies:
+            pl.when(wanted)(copy.wait_recv)
+        down = pltpu.make_async_copy(lists_in, lists_ref, load_sem.at[5])
+        down.start()
+        down.wait()
+        roles = [
+            jnp.where(core == 1, PAIR, SIDE),
+            jnp.where(core == 0, PAIR, SIDE),
+            jnp.where(face == 1, FACE, FAR),
+            jnp.where(face == 0, FACE, FAR),
+        ]
+        for j in range(blocks):
+            table_ref[j] = j
+            last_ref[j] = slot_last_ref[j]
+        for index, role in enumerate(roles):
+            listed = [lists_ref[index, 0, index, e] for e in range(capacity)]
+            ends = [slot_last_ref[blocks + index * capacity + e] for e in range(capacity)]
+            for e in range(capacity):
+                table_ref[blocks + index * capacity + e] = role * blocks + listed[e]
+            for j in range(blocks):
+                end = terms
+                for e in range(capacity):
+                    end = jnp.where(listed[e] == j, ends[e], end)
+                last_ref[role * blocks + j] = end
 
     def field_copy(s, chunk, kind, src_role, dst_role, target):
         return pltpu.make_async_remote_copy(
@@ -159,13 +214,19 @@
 
         lax.fori_loop(0, blocks, body, 0)
 
-    def send_stage(s, chunk):
+    def field_stage(s, chunk):
         field, term = copies(s, chunk)
         start(always, field[FACE])
         start(always, field[PAIR])
+
+    def term_stage(s, chunk):
+        field, term = copies(s, chunk)
         start_row, size = term_rows(s, chunk)
         with_ones = size > part
         rows = pl.ds(start_row, size)
+
+        if with_ones:
+            loads[1].wait()
 
         def row_body(i, carry):
             own = ext[s][chunk][i]
@@ -179,10 +240,18 @@
                 if with_ones:
                     term_now = jnp.concatenate([made[2 * part : 2 * part + 8], term_now], axis=0)
                 at = i * slots + k
-                sums[at, :size] = term_now + sums[before_ref[at], :size]
+                sums[at, :size] = term_now
             return carry
 
-        lax.fori_loop(0, blocks, row_body, 0)
+        lax.fori_loop(0, blocks, row_body, 0, unroll=UNROLL)
+
+        def run_body(at, carry):
+            sums[at, :size] = sums[at, :size] + sums[before_ref[at], :size]
+            return carry
+
+        lax.fori_loop(0, terms, run_body, 0)
+        if with_ones:
+            make_tables()
         for role in (SIDE, FAR, PAIR, FACE):
 
             def pick(j, carry, role=role):
@@ -253,7 +322,7 @@
         def row_body(i, carry):
             made = None
             for k in range(slots):
-                pieces = split_parts(ext[s][chunk][places_ref[i * slots + k]])
+                pieces = split_parts(ext[s][chunk][table_ref[cols_ref[i, k]]])
                 if with_ones:
                     pieces.append(jnp.ones((16, width), jnp.bfloat16))
                 stacked = jnp.concatenate(pieces, axis=0)
@@ -292,7 +361,7 @@
             return carry
 
         zero = jnp.zeros((8, width), f32)
-        return lax.fori_loop(0, blocks, row_body, (zero, zero))
+        return lax.fori_loop(0, blocks, row_body, (zero, zero), unroll=UNROLL)
 
     def reduce_start(index, tiles):
         for n, tile in enumerate(tiles):
@@ -329,19 +398,28 @@
     zero = jnp.zeros((8, width), f32)
     dots = [zero, zero]
     for chunk in range(CHUNKS):
-        send_stage(0, chunk)
+        field_stage(0, chunk)
+    for chunk in range(CHUNKS):
+        term_stage(0, chunk)
+    for load in loads[2:]:
+        load.wait()
     for i in range(blocks):
         seen = mask_ref[:, i, :].astype(f32)
         mask_f[i] = seen
         right[i] = seen * observed_ref[:, i, :]
     for s in range(APPLIED):
+        for stage in (far_terms_stage, face_relay_stage, face_terms_stage, far_relay_stage):
+            for chunk in range(CHUNKS):
+                stage(s, chunk)
         for chunk in range(CHUNKS):
-            relay(s, chunk)
             made = finish_stage(s, chunk)
             if s == 1:
                 dots = [dots[0] + made[0], dots[1] + made[1]]
             if s + 1 < APPLIED:
-                send_stage(s + 1, chunk)
+                field_stage(s + 1, chunk)
+        if s + 1 < APPLIED:
+            for chunk in range(CHUNKS):
+                term_stage(s + 1, chunk)
         if s == 1:
             reduce_start(0, dots)
             norm_first, energy = reduce_done(0, 2)
@@ -382,31 +460,15 @@
         pl.when(cond)(copy.wait_send)
 
 
-def index_tables(block_cols, send_list, blocks):
-    me = lax.axis_index("graph")
-    core, face = me % 2, (me // 2) % 2
-    listed = jnp.stack([shifted(send_list[index], "graph", offset) for index, offset in enumerate(OFFSETS)])
-    role = jnp.stack(
-        [
-            jnp.where(core == 1, PAIR, SIDE),
-            jnp.where(core == 0, PAIR, SIDE),
-            jnp.where(face == 1, FACE, FAR),
-            jnp.where(face == 0, FACE, FAR),
-        ]
-    )
-    received = (role[:, None] * blocks + listed).reshape(-1)
-    table = jnp.concatenate([jnp.arange(blocks, dtype=jnp.int32), received.astype(jnp.int32)])
+def index_tables(block_cols, ext_count):
     flat = block_cols.reshape(-1)
-    places = jnp.sum(jnp.where(flat[:, None] == jnp.arange(table.shape[0])[None], table[None], 0), axis=1)
     terms = flat.shape[0]
-    order = jnp.arange(terms)
-    match = (places[None, :] == places[:, None]) & (order[None, :] < order[:, None])
+    order = jnp.arange(terms, dtype=jnp.int32)
+    match = (flat[None, :] == flat[:, None]) & (order[None, :] < order[:, None])
     before = jnp.max(jnp.where(match, order[None, :], -1), axis=1)
-    hits = places[None, :] == jnp.arange(5 * blocks)[:, None]
+    hits = flat[None, :] == jnp.arange(ext_count, dtype=jnp.int32)[:, None]
     last = jnp.max(jnp.where(hits, order[None, :], -1), axis=1)
-    before = jnp.where(before < 0, terms, before)
-    last = jnp.where(last < 0, terms, last)
-    return places.astype(jnp.int32), before.astype(jnp.int32), last.astype(jnp.int32)
+    return jnp.where(before < 0, terms, before), jnp.where(last < 0, terms, last)
 
 
 def per_device(count, observed, mask, first_guess, diag_weight, coupling, block_cols, send_rows):
@@ -414,7 +476,8 @@
     slots = coupling.shape[1]
     terms = blocks * slots
     part = steps // CHUNKS
-    places, before, last = index_tables(block_cols, send_rows[0], blocks)
+    ext_count = blocks + 4 * send_rows.shape[2]
+    before, last = index_tables(block_cols, ext_count)
     f32 = jnp.float32
     vmem = pl.BlockSpec(memory_space=pltpu.VMEM)
     smem = pl.BlockSpec(memory_space=pltpu.SMEM)
@@ -422,7 +485,7 @@
     return pl.pallas_call(
         functools.partial(cg_kernel, count, blocks, slots, steps),
         out_shape=(shape, shape),
-        in_specs=[smem] * 3 + [vmem] * 5,
+        in_specs=[smem] * 3 + [pl.BlockSpec(memory_space=pl.ANY)] * 6,
         out_specs=(vmem, vmem),
         scratch_shapes=[pltpu.VMEM((5 * blocks, part, width), f32)] * (APPLIED * CHUNKS)
         + [
@@ -436,15 +499,25 @@
             pltpu.VMEM((blocks, 8, width), f32),
             pltpu.VMEM((3, 2, 8, width), f32),
             pltpu.VMEM((3, count - 1, 2, 8, width), f32),
+            pltpu.VMEM(observed.shape, f32),
+            pltpu.VMEM(mask.shape, mask.dtype),
+            pltpu.VMEM(first_guess.shape, f32),
+            pltpu.VMEM(diag_weight.shape, f32),
+            pltpu.VMEM(coupling.shape, coupling.dtype),
+            pltpu.VMEM((4,) + send_rows.shape, jnp.int32),
+            pltpu.SMEM((4,) + send_rows.shape, jnp.int32),
+            pltpu.SMEM((ext_count,), jnp.int32),
+            pltpu.SMEM((5 * blocks,), jnp.int32),
             pltpu.SemaphoreType.DMA((APPLIED, CHUNKS, 8)),
             pltpu.SemaphoreType.DMA((APPLIED, CHUNKS, 8)),
             pltpu.SemaphoreType.DMA((3,)),
             pltpu.SemaphoreType.DMA((3,)),
+            pltpu.SemaphoreType.DMA((14,)),
         ],
         compiler_params=pltpu.CompilerParams(
             collective_id=0, has_side_effects=True, vmem_limit_bytes=48 * 1024 * 1024
         ),
-    )(places, before, last, observed, mask, first_guess, diag_weight, coupling)
+    )(before, last, block_cols, observed, mask, first_guess, diag_weight, coupling, send_rows)
 
 
 def solution(mesh):

time: 123 us -> 94.4 us (0.77)
  Pallas kernels: 101 us -> 84.4 us
  starting transfers between devices: 12.3 us -> 0 us
    pallas_call x1, Pallas kernels: 101 us -> 84.4 us  [per_device(): pl.pallas_call(functools.partial(cg_kernel, count, blocks, slots, steps),...]
    ppermute x4 -> x0, starting transfers between devices: 12.3 us -> none  [shifted(): return lax.ppermute(block, axis, route)]
    unnamed x12 -> x16, local copies, waits for them, and re-layouts: 6.48 us -> 7.84 us
  transfers between devices with their start and end apart: 4 -> 0, of which waited for: 1 -> 0; matrix products, arithmetic and copies ran while one was open for 1% -> 0% of each run, Pallas kernels for 0% -> 0%
where the time goes in v2:
time: 94.4 us; the launch traced here: 94 us
  Pallas kernels  84.4 us (89%)
  local copies, waits for them, and re-layouts  8.61 us (9%)
    pallas_call x1, Pallas kernels, per_device(): pl.pallas_call(functools.partial(cg_kernel, count, blocks, slots, steps),...  84.4 us
    unnamed x16, local copies, waits for them, and re-layouts  7.84 us

profile of v2, /device:TPU:0, one launch (start us, length us, event | category | flops | bytes accessed | tf_op | source)
XLA Modules:
  0.0 94.0 jit_solution(194818817417951901)
XLA Ops:
  0.6 0.8 eq.28
  1.4 0.1 select_reduce_fusion.1
  1.5 0.2 select_reduce_fusion
  1.7 0.0 copy-start
  1.7 1.3 %copy-done = bf16[8,5,128,128]{3,2,1,0:T(8,128)(2,1)S(1)} copy-done((bf16[8,5,128,128]{3,2,1,0:T(8,128)(2,1)S(1)}, bf16[8,5,128,128]{3,2,1,0:T(8,128)(2,1)}, u32[]{:S(2)}) %copy-start) | copy-done | bytes 1310744
  3.0 0.0 copy-start.1
  3.0 1.0 %copy-done.1 = f32[96,8,128]{2,1,0:T(8,128)S(1)} copy-done((f32[96,8,128]{2,1,0:T(8,128)S(1)}, f32[96,8,128]{2,1,0:T(8,128)}, u32[]{:S(2)}) %copy-start.1) | copy-done | bytes 393240
  4.0 0.0 copy-start.2
  4.0 1.0 %copy-done.2 = s32[96,8,128]{2,1,0:T(8,128)S(1)} copy-done((s32[96,8,128]{2,1,0:T(8,128)S(1)}, s32[96,8,128]{2,1,0:T(8,128)}, u32[]{:S(2)}) %copy-start.2) | copy-done | bytes 393240
  5.0 0.0 copy-start.3
  5.0 1.0 %copy-done.3 = f32[96,8,128]{2,1,0:T(8,128)S(1)} copy-done((f32[96,8,128]{2,1,0:T(8,128)S(1)}, f32[96,8,128]{2,1,0:T(8,128)}, u32[]{:S(2)}) %copy-start.3) | copy-done | bytes 393240
  6.0 0.0 copy-start.4
  6.0 0.7 copy-done.4
  6.7 0.0 copy-start.5
  6.7 0.7 copy-done.5
  7.4 0.0 copy-start.6
  7.4 0.7 copy-done.6
  8.1 84.4 %shard_map.86 = (f32[96,8,128]{2,1,0:T(8,128)S(1)}, f32[96,8,128]{2,1,0:T(8,128)S(1)}) custom-call(s32[40]{0:T(128)S(1)} %compare_select_fusion.1.before_ref, s32[24]{0:T(128)S(1)} %compare_select_fusion.slot_last_ref, s32[8,5]{1,0:T(8,128)S(1)} %copy-done.4, f32[96,8,128]{2,1,0:T(8,128)S(1)} %copy-done.1, s32[96,8,128]{2,1,0:T(8,128)S(1)} %copy-done.2, ...), custom_call_target="tpu_custom_call" | custom-call | tf_op jit(solution)/shard_map/pallas_call | solution.py:485
  92.5 0.7 copy.11
  93.2 0.7 copy.12
  (2 shorter events, 0.0 us)
Async XLA Ops:
  1.7 1.3 %copy-start = (bf16[8,5,128,128]{3,2,1,0:T(8,128)(2,1)S(1)}, bf16[8,5,128,128]{3,2,1,0:T(8,128)(2,1)}, u32[]{:S(2)}) copy-start(bf16[8,5,128,128]{3,2,1,0:T(8,128)(2,1)} %weights_hbm.1) | copy-start | bytes 3932164
  3.0 1.0 %copy-start.1 = (f32[96,8,128]{2,1,0:T(8,128)S(1)}, f32[96,8,128]{2,1,0:T(8,128)}, u32[]{:S(2)}) copy-start(f32[96,8,128]{2,1,0:T(8,128)} %observed_hbm.1) | copy-start | bytes 1179652
  4.0 1.0 %copy-start.2 = (s32[96,8,128]{2,1,0:T(8,128)S(1)}, s32[96,8,128]{2,1,0:T(8,128)}, u32[]{:S(2)}) copy-start(s32[96,8,128]{2,1,0:T(8,128)} %mask_hbm.1) | copy-start | bytes 1179652
  5.0 1.0 %copy-start.3 = (f32[96,8,128]{2,1,0:T(8,128)S(1)}, f32[96,8,128]{2,1,0:T(8,128)}, u32[]{:S(2)}) copy-start(f32[96,8,128]{2,1,0:T(8,128)} %guess_hbm.1) | copy-start | bytes 1179652
  6.0 0.7 copy-start.4
  6.7 0.7 copy-start.5
  7.4 0.7 copy-start.6

commit v3 on v2

--- a/solution.py
+++ b/solution.py
@@ -13,6 +13,7 @@
 time_tie = 0.5
 CHUNKS = 2
 UNROLL = 4
+LIMIT = 60
 MESH = pl.DeviceIdType.MESH
 OWN, PAIR, FACE, FAR, SIDE = range(5)
 
@@ -396,11 +397,11 @@
         far_relay_stage(s, chunk)
 
     zero = jnp.zeros((8, width), f32)
-    dots = [zero, zero]
     for chunk in range(CHUNKS):
         field_stage(0, chunk)
     for chunk in range(CHUNKS):
         term_stage(0, chunk)
+        far_terms_stage(0, chunk)
     for load in loads[2:]:
         load.wait()
     for i in range(blocks):
@@ -408,20 +409,9 @@
         mask_f[i] = seen
         right[i] = seen * observed_ref[:, i, :]
     for s in range(APPLIED):
-        for stage in (far_terms_stage, face_relay_stage, face_terms_stage, far_relay_stage):
-            for chunk in range(CHUNKS):
-                stage(s, chunk)
         for chunk in range(CHUNKS):
-            made = finish_stage(s, chunk)
-            if s == 1:
-                dots = [dots[0] + made[0], dots[1] + made[1]]
-            if s + 1 < APPLIED:
-                field_stage(s + 1, chunk)
-        if s + 1 < APPLIED:
-            for chunk in range(CHUNKS):
-                term_stage(s + 1, chunk)
-        if s == 1:
-            reduce_start(0, dots)
+            face_relay_stage(s, chunk)
+        if s == 2:
             norm_first, energy = reduce_done(0, 2)
             step_first = norm_first / energy
 
@@ -433,8 +423,21 @@
                 return carry
 
             reduce_start(1, [lax.fori_loop(0, blocks, next_residual, zero)])
-            (norm_second,) = reduce_done(1, 1)
-            ratio = norm_second / norm_first
+        for chunk in range(CHUNKS):
+            face_terms_stage(s, chunk)
+            far_relay_stage(s, chunk)
+        dots = [zero, zero]
+        for chunk in range(CHUNKS):
+            made = finish_stage(s, chunk)
+            dots = [dots[0] + made[0], dots[1] + made[1]]
+            if s + 1 < APPLIED:
+                field_stage(s + 1, chunk)
+                if s == 1 and chunk == CHUNKS - 1:
+                    reduce_start(0, dots)
+                term_stage(s + 1, chunk)
+                far_terms_stage(s + 1, chunk)
+    (norm_second,) = reduce_done(1, 1)
+    ratio = norm_second / norm_first
 
     def last_dot(i, carry):
         for chunk in range(CHUNKS):
@@ -515,7 +518,7 @@
             pltpu.SemaphoreType.DMA((14,)),
         ],
         compiler_params=pltpu.CompilerParams(
-            collective_id=0, has_side_effects=True, vmem_limit_bytes=48 * 1024 * 1024
+            collective_id=0, has_side_effects=True, vmem_limit_bytes=LIMIT * 1024 * 1024
         ),
     )(before, last, block_cols, observed, mask, first_guess, diag_weight, coupling, send_rows)
 

time: 94.4 us -> 83.3 us (0.88)
  Pallas kernels: 84.4 us -> 76.7 us
  local copies, waits for them, and re-layouts: 8.61 us -> 4.3 us
  other arithmetic: 0.31 us -> 1.33 us
    pallas_call x1, Pallas kernels: 84.4 us -> 76.7 us  [per_device(): pl.pallas_call(functools.partial(cg_kernel, count, blocks, slots, steps),...]
    unnamed x16 -> x2, local copies, waits for them, and re-layouts: 7.84 us -> 3.53 us
where the time goes in v3:
time: 83.3 us; the launch traced here: 83 us
  Pallas kernels  76.7 us (92%)
  local copies, waits for them, and re-layouts  4.3 us (5%)
  other arithmetic  1.33 us (2%)
    pallas_call x1, Pallas kernels, per_device(): pl.pallas_call(functools.partial(cg_kernel, count, blocks, slots, steps),...  76.7 us
    unnamed x2, local copies, waits for them, and re-layouts  3.53 us

profile of v3, /device:TPU:0, one launch (start us, length us, event | category | flops | bytes accessed | tf_op | source)
XLA Modules:
  0.0 83.0 jit_solution(11617834121963739721)
XLA Ops:
  0.6 0.8 eq.28
  1.4 0.1 select_reduce_fusion.1
  1.5 0.2 select_reduce_fusion
  1.7 0.5 compare_select_fusion.1.before_ref
  2.2 0.5 compare_select_fusion.slot_last_ref
  2.7 76.7 %shard_map.86 = (f32[96,8,128]{2,1,0:T(8,128)}, f32[96,8,128]{2,1,0:T(8,128)}) custom-call(s32[40]{0:T(128)} %compare_select_fusion.1.before_ref, s32[24]{0:T(128)} %compare_select_fusion.slot_last_ref, s32[8,5]{1,0:T(8,128)} %cols_ref.1, f32[96,8,128]{2,1,0:T(8,128)} %observed_hbm.1, s32[96,8,128]{2,1,0:T(8,128)} %mask_hbm.1, f32[96,8,128]{2,1,0:T(8,128)} %guess_hbm.1, ...), custom_call_target="tpu_custom_call" | custom-call | tf_op jit(solution)/shard_map/pallas_call | solution.py:488
  79.5 1.8 %copy.11 = f32[96,8,128]{2,1,0:T(8,128)} copy(f32[96,8,128]{2,1,0:T(8,128)} %get-tuple-element.4) | data formatting | bytes 786432
  81.3 1.8 %copy.12 = f32[96,8,128]{2,1,0:T(8,128)} copy(f32[96,8,128]{2,1,0:T(8,128)} %get-tuple-element.5) | data formatting | bytes 786432

commit v4 on v3

--- a/solution.py
+++ b/solution.py
@@ -54,7 +54,7 @@
     *scratch,
 ):
     ext = [scratch[s * CHUNKS : (s + 1) * CHUNKS] for s in range(APPLIED)]
-    final, mask_f, right, sums, kept, out_terms, in_terms, diag, red_out, red_in = scratch[APPLIED * CHUNKS : -14]
+    final, mask_f, right, forward, sums, kept, out_terms, in_terms, diag, red_out, red_in = scratch[APPLIED * CHUNKS : -14]
     observed_ref, mask_ref, guess_ref, prior_ref, weights_ref, lists_in, lists_ref, table_ref, last_ref = scratch[-14:-5]
     send_sem, recv_sem, red_send_sem, red_recv_sem, load_sem = scratch[-5:]
     width = guess_ref.shape[2]
@@ -213,7 +213,7 @@
             out_terms[s, at, rows] = out_terms[s, at, rows] + in_terms[s, (other - 1) * blocks + j, rows]
             return carry
 
-        lax.fori_loop(0, blocks, body, 0)
+        lax.fori_loop(0, blocks, body, 0, unroll=2 * UNROLL)
 
     def field_stage(s, chunk):
         field, term = copies(s, chunk)
@@ -250,7 +250,7 @@
             sums[at, :size] = sums[at, :size] + sums[before_ref[at], :size]
             return carry
 
-        lax.fori_loop(0, terms, run_body, 0)
+        lax.fori_loop(0, terms, run_body, 0, unroll=2 * UNROLL)
         if with_ones:
             make_tables()
         for role in (SIDE, FAR, PAIR, FACE):
@@ -259,7 +259,7 @@
                 out_terms[s, (role - 1) * blocks + j, rows] = sums[last_ref[role * blocks + j], :size]
                 return carry
 
-            lax.fori_loop(0, blocks, pick, 0)
+            lax.fori_loop(0, blocks, pick, 0, unroll=2 * UNROLL)
             if role == SIDE:
                 start(jnp.logical_not(same) | has_src, term[SIDE])
             if role == FAR:
@@ -271,7 +271,7 @@
             kept[s, j, rows] = sums[last_ref[j], :size]
             return carry
 
-        lax.fori_loop(0, blocks, keep, 0)
+        lax.fori_loop(0, blocks, keep, 0, unroll=2 * UNROLL)
 
     def far_terms_stage(s, chunk):
         field, term = copies(s, chunk)
@@ -310,15 +310,12 @@
         arrived(has_src, field[FAR])
         start(jnp.logical_not(same) & has_src, field["other"])
 
-    def finish_stage(s, chunk):
-        field, term = copies(s, chunk)
-        start_row, size = term_rows(s, chunk)
-        with_ones = size > part
+    def forward_stage(s, chunk):
+        field, term = copies(s, chunk)
+        with_ones = s == 0 and chunk == 0
         here = pl.ds(chunk * part, part)
         arrived(always, field[PAIR])
         arrived(jnp.logical_not(same) | has_src, field[SIDE])
-        arrived(always, term[PAIR])
-        arrived(always, term[FACE])
 
         def row_body(i, carry):
             made = None
@@ -331,6 +328,22 @@
                     stacked, weights_ref[i, k], (((1,), (1,)), ((), ())), preferred_element_type=f32
                 )
                 made = product if made is None else made + product
+            if with_ones:
+                diag[i] = made[2 * part : 2 * part + 8] + prior_ref[pl.ds(i, 1), :]
+            forward[i, here] = made[:part] + made[part : 2 * part]
+            return carry
+
+        lax.fori_loop(0, blocks, row_body, 0, unroll=UNROLL)
+
+    def finish_stage(s, chunk):
+        field, term = copies(s, chunk)
+        start_row, size = term_rows(s, chunk)
+        with_ones = size > part
+        here = pl.ds(chunk * part, part)
+        arrived(always, term[PAIR])
+        arrived(always, term[FACE])
+
+        def row_body(i, carry):
             trows = pl.ds(start_row, size)
             returned = (
                 kept[s, i, trows]
@@ -338,9 +351,9 @@
                 + in_terms[s, (FACE - 1) * blocks + i, trows]
             )
             if with_ones:
-                diag[i] = made[2 * part : 2 * part + 8] + returned[:8] + prior_ref[pl.ds(i, 1), :]
+                diag[i] = diag[i] + returned[:8]
                 returned = returned[8:]
-            coupled = made[:part] + made[part : 2 * part] + returned
+            coupled = forward[i, here] + returned
             now = ext[s][chunk][i]
             if chunk == 0:
                 earlier = jnp.concatenate([now[:1], now[:-1]], axis=0)
@@ -426,8 +439,12 @@
         for chunk in range(CHUNKS):
             face_terms_stage(s, chunk)
             far_relay_stage(s, chunk)
+            if chunk == 0:
+                forward_stage(s, chunk)
         dots = [zero, zero]
         for chunk in range(CHUNKS):
+            if chunk > 0:
+                forward_stage(s, chunk)
             made = finish_stage(s, chunk)
             dots = [dots[0] + made[0], dots[1] + made[1]]
             if s + 1 < APPLIED:
@@ -492,6 +509,7 @@
         out_specs=(vmem, vmem),
         scratch_shapes=[pltpu.VMEM((5 * blocks, part, width), f32)] * (APPLIED * CHUNKS)
         + [
+            pltpu.VMEM((blocks, steps, width), f32),
             pltpu.VMEM((blocks, steps, width), f32),
             pltpu.VMEM((blocks, steps, width), f32),
             pltpu.VMEM((blocks, steps, width), f32),

time: 83.3 us -> 81.7 us (0.981)
  Pallas kernels: 76.7 us -> 75.2 us
    pallas_call x1, Pallas kernels: 76.7 us -> 75.2 us  [per_device(): pl.pallas_call(functools.partial(cg_kernel, count, blocks, slots, steps),...]
where the time goes in v4:
time: 81.7 us; the launch traced here: 81.5 us
  Pallas kernels  75.2 us (92%)
  local copies, waits for them, and re-layouts  4.3 us (5%)
  other arithmetic  1.33 us (2%)
    pallas_call x1, Pallas kernels, per_device(): pl.pallas_call(functools.partial(cg_kernel, count, blocks, slots, steps),...  75.2 us
    unnamed x2, local copies, waits for them, and re-layouts  3.53 us

profile of v4, /device:TPU:0, one launch (start us, length us, event | category | flops | bytes accessed | tf_op | source)
XLA Modules:
  0.0 81.5 jit_solution(3994476584228057551)
XLA Ops:
  0.6 0.8 eq.28
  1.4 0.1 select_reduce_fusion.1
  1.5 0.2 select_reduce_fusion
  1.7 0.5 compare_select_fusion.1.before_ref
  2.2 0.5 compare_select_fusion.slot_last_ref
  2.7 75.2 %shard_map.86 = (f32[96,8,128]{2,1,0:T(8,128)}, f32[96,8,128]{2,1,0:T(8,128)}) custom-call(s32[40]{0:T(128)} %compare_select_fusion.1.before_ref, s32[24]{0:T(128)} %compare_select_fusion.slot_last_ref, s32[8,5]{1,0:T(8,128)} %cols_ref.1, f32[96,8,128]{2,1,0:T(8,128)} %observed_hbm.1, s32[96,8,128]{2,1,0:T(8,128)} %mask_hbm.1, f32[96,8,128]{2,1,0:T(8,128)} %guess_hbm.1, ...), custom_call_target="tpu_custom_call" | custom-call | tf_op jit(solution)/shard_map/pallas_call | solution.py:505
  77.9 1.8 %copy.11 = f32[96,8,128]{2,1,0:T(8,128)} copy(f32[96,8,128]{2,1,0:T(8,128)} %get-tuple-element.4) | data formatting | bytes 786432
  79.7 1.8 %copy.12 = f32[96,8,128]{2,1,0:T(8,128)} copy(f32[96,8,128]{2,1,0:T(8,128)} %get-tuple-element.5) | data formatting | bytes 786432
